TPU v7x, 256 devices: a whole 4x4x8 slice. The times are simulated.
256 devices in a mesh: occ: 32 (over y, x, core), pts: 8 (over z).
Axes of the slice: x: 4, y: 4, z: 8, core: 2. Of those that a mesh axis runs over, the one named last changes fastest.
Arguments:
- integrals: bfloat16 [32, 1024, 4608], P(None, 'occ'), may hold values from -0.0029296875 to 0.0029296875
- occupied_points: bfloat16 [1024, 6144], P('occ', 'pts'), may hold values from -6 to 6
- virtual_points: bfloat16 [4608, 6144], P('occ', 'pts'), may hold values from -6 to 6
Outputs:
- gram: float32 [6144, 6144], P('pts', 'occ')
All inputs are finite; a program needn't handle non-finite values.
Results may differ from a plain program's by a relative error of at most 0.0003.
Values may be sent and summed in bfloat16 or wider, within the bound.
A program may use at most 128 MiB of HBM per device.

v0:
```python
import jax
import jax.numpy as jnp
from jax import lax
from jax.sharding import PartitionSpec as P


def body(integrals, occupied_points, virtual_points):
    naux, occ_local, nvirt = integrals.shape
    npts_local = virtual_points.shape[1]
    flat_rows = integrals.reshape(naux * occ_local, nvirt)
    contracted = jnp.dot(
        flat_rows,
        lax.all_gather(virtual_points, "occ", axis=0, tiled=True),
        preferred_element_type=jnp.float32,
    )
    contracted = contracted.reshape(naux, occ_local, npts_local)
    partial_y = jnp.sum(contracted * occupied_points.astype(jnp.float32)[None], axis=1)
    projection = lax.psum(partial_y, "occ")
    tile_width = npts_local * lax.axis_size("pts") // lax.axis_size("occ")
    column_start = lax.axis_index("occ") * tile_width
    whole_panel = lax.all_gather(projection, "pts", axis=1, tiled=True)
    tile_columns = lax.dynamic_slice_in_dim(whole_panel, column_start, tile_width, 1)
    return lax.dot_general(
        projection,
        tile_columns,
        (((0,), (0,)), ((), ())),
        precision=lax.Precision.HIGHEST,
        preferred_element_type=jnp.float32,
    )


def solution(mesh):
    return jax.shard_map(
        body,
        mesh=mesh,
        in_specs=(P(None, "occ", None), P("occ", "pts"), P("occ", "pts")),
        out_specs=P("pts", "occ"),
        check_vma=False,
    )
```

profile of v0, /device:TPU:2, one launch (start us, length us, event | category | flops | bytes accessed | tf_op | source)
XLA Modules:
  0.0 225.6 jit_solution(7099347241526233215)
XLA Ops:
  6.5 0.0 all-gather.2.cloned.1.call-start
  6.5 0.7 all-gather.2.cloned.1.call-update
  7.3 0.0 all-reduce.2.cloned.1.call-start
  7.3 0.8 convert_element_type.3
  8.1 59.7 %all-gather.2.cloned.1.call-done = bf16[4608,768]{1,0:T(8,128)(2,1)} async-done(((bf16[144,768]{1,0:T(8,128)(2,1)}), bf16[4608,768]{1,0:T(8,128)(2,1)}) %all-gather.2.cloned.1.call-update) | async-done | bytes 7077904 | tf_op jit(solution)/shard_map/all_gather | solution.py:13
  67.8 12.8 %multiply_reduce_fusion = f32[32,768]{1,0:T(8,128)} fusion(bf16[32,32,4608]{2,1,0:T(8,128)(2,1)} %param.3, bf16[4608,768]{1,0:T(8,128)(2,1)} %all-gather.2.cloned.1.call-done, f32[32,768]{1,0:T(8,128)S(1)} %convert_element_type.3), kind=kOutput, calls=%fused_computation.2 | convolution fusion | flops 7249305600 | bytes 16711680 | tf_op jit(solution)/shard_map/dot_general | solution.py:11
  80.5 0.0 all-reduce.2.cloned.1.call-update
  80.6 107.8 %all-reduce.2.cloned.1.call-done = f32[32,768]{1,0:T(8,128)} async-done(((f32[32,768]{1,0:T(8,128)}), f32[32,768]{1,0:T(8,128)}) %all-reduce.2.cloned.1.call-update) | async-done | bytes 98320 | tf_op jit(solution)/shard_map/psum | solution.py:18
  188.4 28.0 %all_gather.7 = f32[32,6144]{1,0:T(8,128)S(1)} all-gather(f32[32,768]{1,0:T(8,128)} %all-reduce.2.cloned.1.call-done), channel_id=1, replica_groups=mesh['occ'=32,'pts'=8] {'pts'}, dimensions={1}, use_global_device_ids=true | all-gather | bytes 884736 | tf_op jit(solution)/shard_map/all_gather | solution.py:21
  216.4 2.4 %fusion.4 = f32[768,192]{0,1:T(8,128)} fusion(f32[32,768]{1,0:T(8,128)} %all-reduce.2.cloned.1.call-done, f32[32,6144]{1,0:T(8,128)S(1)} %all_gather.7, s32[]{:T(128)S(6)} %select_n.3), kind=kOutput, calls=%fused_computation.3 | convolution fusion | flops 56623104 | bytes 720900 | tf_op jit(solution)/shard_map/dot_general | solution.py:23
Async XLA Ops:
  6.5 61.3 %all-gather.2.cloned.1.call-start = ((), (), s32[]{:S(2)}) async-start(), calls=%async_computation | async-start | bytes 7299072 | tf_op jit(solution)/shard_map/all_gather | solution.py:13
  7.3 181.1 %all-reduce.2.cloned.1.call-start = ((), (), s32[]{:S(2)}) async-start(), calls=%async_computation.1 | async-start | bytes 196608 | tf_op jit(solution)/shard_map/psum | solution.py:18
Sparse Core Ops, SparseCore 0:
  9.9 57.8 all-gather.1
  80.7 107.6 all-reduce.1
where the time goes:
time: 226 us
  waiting for transfers between devices  168 us (74%)
  blocking collectives  28 us (12%)
  matrix products  15.2 us (7%)
  between operations  13.4 us (6%)
    psum x1, waiting for transfers between devices, body(): projection = lax.psum(partial_y, 'occ')  108 us
    all_gather x1, waiting for transfers between devices, body(): lax.all_gather(virtual_points, 'occ', axis=0, tiled=True)  59.7 us
    all_gather x1, blocking collectives, body(): whole_panel = lax.all_gather(projection, 'pts', axis=1, tiled=True)  28 us
    dot_general x1, matrix products, body(): jnp.dot(flat_rows, lax.all_gather(virtual_points, 'occ', axis=0, tiled=Tr...  12.8 us
  transfers between devices with their start and end apart: 2, of which 2 were waited for; matrix products, arithmetic and copies ran while one was open for 0% of the time, Pallas kernels for 0%

commit v1 on v0

v1 whole, which is shorter than its diff:
```python
import functools

import jax
import jax.numpy as jnp
from jax import lax
from jax.experimental import pallas as pl
from jax.experimental.pallas import tpu as pltpu
from jax.sharding import PartitionSpec as P

MESH = pl.DeviceIdType.MESH
NX, NY, NZ = 4, 4, 8
PLANE = NX * NY * 2
CHUNK = 256
LANES = 128
TILE_P = 8


def split3(x):
    hi = x.astype(jnp.bfloat16)
    rest = x - hi.astype(jnp.float32)
    mid = rest.astype(jnp.bfloat16)
    low = (rest - mid.astype(jnp.float32)).astype(jnp.bfloat16)
    return hi, mid, low


def kernel(b_hbm, occ_hbm, v_hbm, out_ref, b_ref, occ_ref, panel, part, gathered, total, rows_y, cols_y,
           local_sem, recv_sem, send_sem, rs_send, rs_recv, ag_send, ag_recv, col_recv):
    nrows, width = v_hbm.shape
    nchunks = width // CHUNK
    tiles_q = width // LANES
    naux = part.shape[1]
    groups = naux // TILE_P
    owners = tiles_q * groups
    occ_local = occ_ref.shape[0]

    me = lax.axis_index("occ")
    z = lax.axis_index("pts")
    core = lax.rem(me, 2)
    x = lax.rem(me // 2, NX)
    y = me // (2 * NX)
    first = x + core * (y - x)
    second = y + core * (x - y)

    def occ_of(f, s):
        f = lax.rem(first + f + 4, 4)
        s = lax.rem(second + s + 4, 4)
        return (s * (4 - 3 * core) + f * (1 + 3 * core)) * 2 + core

    def at(f, s):
        return {"occ": occ_of(f, s), "pts": z}

    sibling = {"occ": me + 1 - 2 * core, "pts": z}

    home = me // 4
    tile = lax.rem(me, 4)
    first_block = 3 * (tile // 2) + lax.rem(tile, 2)
    is_home = home == z
    is_owner = me < owners
    my_block = me // groups
    my_group = lax.rem(me, groups)
    both = lax.rem(my_block, 3) == 1

    barrier = pltpu.get_barrier_semaphore()

    def greet(n, _):
        pl.semaphore_signal(barrier, inc=1, device_id={"occ": lax.rem(me + n, PLANE), "pts": z}, device_id_type=MESH)
        return 0

    lax.fori_loop(1, PLANE, greet, 0)

    @pl.when(jnp.logical_not(is_home))
    def _():
        def greet_owner(n, _):
            pl.semaphore_signal(
                barrier, inc=1, device_id={"occ": first_block * groups + n, "pts": home}, device_id_type=MESH
            )
            return 0

        lax.fori_loop(0, 2 * groups, greet_owner, 0)

    b_copy = pltpu.make_async_copy(b_hbm, b_ref, local_sem.at[0])
    occ_copy = pltpu.make_async_copy(occ_hbm, occ_ref, local_sem.at[1])
    own_copies = [
        pltpu.make_async_copy(
            v_hbm.at[:, pl.ds(k * CHUNK, CHUNK)], panel.at[k, pl.ds(me * nrows, nrows)], local_sem.at[2 + k]
        )
        for k in range(nchunks)
    ]
    for copy in own_copies:
        copy.start()
    b_copy.start()
    occ_copy.start()

    peers = PLANE - 1 + jnp.where(is_owner, (NZ - 1) * jnp.where(both, 2, 1), 0)
    pl.semaphore_wait(barrier, peers)

    half = nrows // 32 * 16 + 16 if nrows % 32 else nrows // 2

    def push(k, row, count, device, slot, src=None):
        block = panel.at[k, pl.ds(row, count)]
        pltpu.make_async_remote_copy(
            src_ref=block if src is None else src,
            dst_ref=block,
            send_sem=send_sem.at[k],
            recv_sem=recv_sem.at[k, slot],
            device_id=device,
            device_id_type=MESH,
        ).start()

    def row_of(f, s):
        return pl.multiple_of(occ_of(f, s) * nrows, 16)

    def shard(k, f, s, device, slot):
        push(k, row_of(f, s), nrows, device, slot)

    def arrived(k, slot, count):
        block = panel.at[k, pl.ds(0, count)]
        pltpu.make_async_copy(block, block, recv_sem.at[k, slot]).wait()

    def phase0(k):
        src = v_hbm.at[:, pl.ds(k * CHUNK, CHUNK)]
        row = row_of(0, 0)
        push(k, row, nrows, at(1, 0), 0, src)
        push(k, row, nrows, at(-1, 0), 1, src)
        push(k, row, nrows, sibling, 10, src)

    def phase1(k):
        own_copies[k].wait()
        arrived(k, 0, nrows)
        push(k, row_of(-1, 0), half, at(1, 0), 2)
        arrived(k, 1, nrows)
        push(k, pl.multiple_of(row_of(1, 0) + half, 16), nrows - half, at(-1, 0), 3)
        for f in (0, -1):
            shard(k, f, 0, at(0, 1), 4)
        shard(k, 1, 0, at(0, -1), 6)
        shard(k, 1, 0, at(0, 1), 5)
        for f in (0, -1):
            shard(k, f, 0, at(0, -1), 7)
        shard(k, 1, 0, sibling, 10)
        shard(k, -1, 0, sibling, 10)

    def phase2(k):
        arrived(k, 2, half)
        arrived(k, 3, nrows - half)
        shard(k, 2, 0, at(0, -1), 6)
        shard(k, 2, 0, at(0, 1), 5)
        shard(k, 2, 0, sibling, 10)

    def phase3a(k):
        arrived(k, 4, 2 * nrows)
        for f in (0, -1):
            shard(k, f, -1, at(0, 1), 8)
        arrived(k, 6, 2 * nrows)
        for f in (1, 2):
            shard(k, f, 1, at(0, -1), 9)
        for f in (0, -1):
            shard(k, f, -1, sibling, 10)
        for f in (1, 2):
            shard(k, f, 1, sibling, 10)

    def phase3b(k):
        arrived(k, 5, 2 * nrows)
        for f in (1, 2):
            shard(k, f, -1, sibling, 10)
        arrived(k, 7, 2 * nrows)
        for f in (0, -1):
            shard(k, f, 1, sibling, 10)

    def phase4(k):
        arrived(k, 8, 2 * nrows)
        for f in (0, -1):
            shard(k, f, 2, sibling, 10)
        arrived(k, 9, 2 * nrows)
        for f in (1, 2):
            shard(k, f, 2, sibling, 10)

    def phase5(k):
        arrived(k, 10, PLANE // 2 * nrows)

    def send_tile(qb, g):
        owner = qb * groups + g

        @pl.when(me != owner)
        def _():
            pltpu.make_async_remote_copy(
                src_ref=part.at[qb, pl.ds(g * TILE_P, TILE_P)],
                dst_ref=gathered.at[lax.rem(me - owner + PLANE, PLANE) - 1],
                send_sem=rs_send,
                recv_sem=rs_recv,
                device_id={"occ": owner, "pts": z},
                device_id_type=MESH,
            ).start()

    def compute(k, g):
        depth = TILE_P * occ_local
        t = jnp.dot(b_ref[pl.ds(g * depth, depth), :], panel[k], preferred_element_type=jnp.float32)
        o = occ_ref[:, pl.ds(k * CHUNK, CHUNK)].astype(jnp.float32)
        sums = jnp.sum(t.reshape(TILE_P, occ_local, CHUNK) * o[None], axis=1)
        for h in range(CHUNK // LANES):
            part[k * (CHUNK // LANES) + h, pl.ds(g * TILE_P, TILE_P)] = sums[:, h * LANES:(h + 1) * LANES]
        for h in range(CHUNK // LANES):
            send_tile(k * (CHUNK // LANES) + h, g)

    for k in range(nchunks):
        phase0(k)
    phase1(0)
    phase2(0)
    phase1(1)
    phase2(1)
    phase3a(0)
    phase3b(0)
    phase1(2)
    phase2(2)
    phase4(0)
    b_copy.wait()
    occ_copy.wait()
    phase5(0)
    compute(0, 0)
    phase3a(1)
    compute(0, 1)
    phase3b(1)
    compute(0, 2)
    compute(0, 3)
    phase4(1)
    phase3a(2)
    phase5(1)
    compute(1, 0)
    phase3b(2)
    compute(1, 1)
    compute(1, 2)
    compute(1, 3)
    phase4(2)
    phase5(2)
    for g in range(groups):
        compute(2, g)

    def rs_bytes(count):
        block = gathered.at[pl.ds(0, count)]
        pltpu.make_async_copy(block, block, rs_recv).wait()

    @pl.when(is_owner)
    def _():
        rs_bytes(PLANE - 1)
        acc = part[my_block, pl.ds(pl.multiple_of(my_group * TILE_P, TILE_P), TILE_P)]
        for n in range(PLANE - 1):
            acc = acc + gathered[n]
        total[...] = acc
        rows_y[my_block, pl.ds(pl.multiple_of(my_group * TILE_P, TILE_P), TILE_P)] = acc

        def to_column(tile_index):
            slot = my_block - (3 * (tile_index // 2) + lax.rem(tile_index, 2))

            def send(n, _):
                pltpu.make_async_remote_copy(
                    src_ref=total,
                    dst_ref=cols_y.at[slot, pl.ds(pl.multiple_of(my_group * TILE_P, TILE_P), TILE_P)],
                    send_sem=ag_send,
                    recv_sem=col_recv,
                    device_id={"occ": z * 4 + tile_index, "pts": lax.rem(z + n, NZ)},
                    device_id_type=MESH,
                ).start()
                return 0

            lax.fori_loop(1, NZ, send, 0)

        low_tile = 2 * (my_block // 3) + lax.rem(my_block, 3) // 2
        to_column(low_tile)

        @pl.when(both)
        def _():
            to_column(low_tile + 1)

        def to_plane(n, _):
            pltpu.make_async_remote_copy(
                src_ref=total,
                dst_ref=rows_y.at[my_block, pl.ds(pl.multiple_of(my_group * TILE_P, TILE_P), TILE_P)],
                send_sem=ag_send,
                recv_sem=ag_recv,
                device_id={"occ": lax.rem(me + n, PLANE), "pts": z},
                device_id_type=MESH,
            ).start()
            return 0

        lax.fori_loop(1, PLANE, to_plane, 0)

    def wait_tiles(sem, count):
        block = gathered.at[pl.ds(0, count)]
        pltpu.make_async_copy(block, block, sem).wait()

    @pl.when(is_owner)
    def _():
        wait_tiles(ag_recv, owners - 1)

    @pl.when(jnp.logical_not(is_owner))
    def _():
        wait_tiles(ag_recv, owners)

    @pl.when(is_home)
    def _():
        cols_y[...] = rows_y[pl.ds(first_block, 2)]

    @pl.when(jnp.logical_not(is_home))
    def _():
        wait_tiles(col_recv, 2 * groups)

    odd = lax.rem(me, 2) == 1
    cols = jnp.concatenate([cols_y[0], cols_y[1]], axis=1)
    cols = jnp.where(odd, pltpu.roll(cols, cols.shape[1] - LANES // 2, 1), cols)
    c1, c2, c3 = split3(cols)
    right = jnp.concatenate([c1, c2, c1, c2, c3, c1], axis=0)
    for qb in range(tiles_q):
        r1, r2, r3 = split3(rows_y[qb])
        left = jnp.concatenate([r1, r1, r2, r2, r1, r3], axis=0)
        g = lax.dot_general(left, right, (((0,), (0,)), ((), ())), preferred_element_type=jnp.float32)
        out_ref[pl.ds(qb * LANES, LANES), :] = g[:, :out_ref.shape[1]]

    for k in range(nchunks):
        sent = panel.at[k, pl.ds(0, (PLANE - 1) * nrows)]
        pltpu.make_async_copy(sent, sent, send_sem.at[k]).wait()

    @pl.when(is_owner)
    def _():
        wait_tiles(rs_send, owners - 1)
        wait_tiles(ag_send, PLANE - 1)
        wait_tiles(ag_send, NZ - 1)

        @pl.when(both)
        def _():
            wait_tiles(ag_send, NZ - 1)

    @pl.when(jnp.logical_not(is_owner))
    def _():
        wait_tiles(rs_send, owners)


def body(integrals, occupied_points, virtual_points):
    naux, occ_local, nvirt = integrals.shape
    nrows, width = virtual_points.shape
    nchunks = width // CHUNK
    tiles_q = width // LANES
    tile_width = width * NZ // PLANE
    flat = integrals.reshape(naux * occ_local, nvirt)
    anywhere = pl.BlockSpec(memory_space=pl.ANY)
    return pl.pallas_call(
        kernel,
        out_shape=jax.ShapeDtypeStruct((width, tile_width), jnp.float32),
        in_specs=[anywhere] * 3,
        out_specs=pl.BlockSpec(memory_space=pltpu.VMEM),
        scratch_shapes=[
            pltpu.VMEM((naux * occ_local, nvirt), jnp.bfloat16),
            pltpu.VMEM((occ_local, width), jnp.bfloat16),
            pltpu.VMEM((nchunks, nvirt, CHUNK), jnp.bfloat16),
            pltpu.VMEM((tiles_q, naux, LANES), jnp.float32),
            pltpu.VMEM((PLANE, TILE_P, LANES), jnp.float32),
            pltpu.VMEM((TILE_P, LANES), jnp.float32),
            pltpu.VMEM((tiles_q, naux, LANES), jnp.float32),
            pltpu.VMEM((2, naux, LANES), jnp.float32),
            pltpu.SemaphoreType.DMA((2 + nchunks,)),
            pltpu.SemaphoreType.DMA((nchunks, 11)),
            pltpu.SemaphoreType.DMA((nchunks,)),
            pltpu.SemaphoreType.DMA,
            pltpu.SemaphoreType.DMA,
            pltpu.SemaphoreType.DMA,
            pltpu.SemaphoreType.DMA,
            pltpu.SemaphoreType.DMA,
        ],
        compiler_params=pltpu.CompilerParams(
            collective_id=0, has_side_effects=True, vmem_limit_bytes=56 * 2**20
        ),
        cost_estimate=pl.CostEstimate(
            flops=2 * naux * occ_local * nvirt * width, bytes_accessed=12 * 2**20, transcendentals=0
        ),
    )(flat, occupied_points, virtual_points)


def solution(mesh):
    return jax.shard_map(
        body,
        mesh=mesh,
        in_specs=(P(None, "occ", None), P("occ", "pts"), P("occ", "pts")),
        out_specs=P("pts", "occ"),
        check_vma=False,
    )
```

time: 226 us -> 61.8 us (0.27)
  the two profiles are of different devices: /device:TPU:2 before, /device:TPU:1 now
where the time goes in v1:
time: 61.8 us; the launch traced here: 61.7 us
  Pallas kernels  59.4 us (96%)
  local copies, waits for them, and re-layouts  2.2 us (4%)
    pallas_call x1, Pallas kernels, body(): pl.pallas_call(kernel, out_shape=jax.ShapeDtypeStruct((width, tile_width)...  59.4 us
    pallas_call x1, local copies, waits for them, and re-layouts, body(): pl.pallas_call(kernel, out_shape=jax.ShapeDtypeStruct((width, tile_width)...  2.2 us

profile of v1, /device:TPU:1, one launch (start us, length us, event | category | flops | bytes accessed | tf_op | source)
XLA Modules:
  0.0 61.7 jit_solution(16129713858451408317)
XLA Ops:
  0.0 59.4 %shard_map.37 = f32[768,192]{1,0:T(8,128)} custom-call(bf16[1024,4608]{1,0:T(8,128)(2,1)} %bitcast.1, bf16[32,768]{1,0:T(8,128)(2,1)} %occ_hbm.1, bf16[144,768]{1,0:T(8,128)(2,1)} %v_hbm.1), custom_call_target="tpu_custom_call" | custom-call | flops 7247757312 | bytes 12582912 | tf_op jit(solution)/shard_map/pallas_call | solution.py:344
  59.5 2.2 %copy.4 = f32[768,192]{0,1:T(8,128)} copy(f32[768,192]{1,0:T(8,128)} %shard_map.37) | data formatting | bytes 1179648 | tf_op jit(solution)/shard_map/pallas_call | solution.py:344

commit v2 on v1

v2 whole, which is shorter than its diff:
```python
import functools

import jax
import jax.numpy as jnp
from jax import lax
from jax.experimental import pallas as pl
from jax.experimental.pallas import tpu as pltpu
from jax.sharding import PartitionSpec as P

MESH = pl.DeviceIdType.MESH
NX, NY, NZ = 4, 4, 8
PLANE = NX * NY * 2
CHUNK = 256
LANES = 128
TILE_P = 8


def split3(x):
    hi = x.astype(jnp.bfloat16)
    rest = x - hi.astype(jnp.float32)
    mid = rest.astype(jnp.bfloat16)
    low = (rest - mid.astype(jnp.float32)).astype(jnp.bfloat16)
    return hi, mid, low


def kernel(b_hbm, occ_hbm, v_hbm, rows_y, cols_y, b_ref, occ_ref, panel, part, gathered, total,
           local_sem, recv_sem, send_sem, rs_send, rs_recv, ag_send, ag_recv, col_recv, z_token):
    nrows, width = v_hbm.shape
    nchunks = width // CHUNK
    blocks = CHUNK // LANES
    naux = part.shape[1]
    groups = naux // TILE_P
    tiles = blocks * groups
    last = nchunks - 1
    occ_local = occ_ref.shape[0]

    me = lax.axis_index("occ")
    z = lax.axis_index("pts")
    core = lax.rem(me, 2)
    x = lax.rem(me // 2, NX)
    y = me // (2 * NX)
    first = x + core * (y - x)
    second = y + core * (x - y)

    def occ_of(f, s):
        f = lax.rem(first + f + 4, 4)
        s = lax.rem(second + s + 4, 4)
        return (s * (4 - 3 * core) + f * (1 + 3 * core)) * 2 + core

    def at(f, s):
        return {"occ": occ_of(f, s), "pts": z}

    sibling = {"occ": me + 1 - 2 * core, "pts": z}
    above = {"occ": me, "pts": lax.rem(z + 1, NZ)}
    below = {"occ": me, "pts": lax.rem(z + NZ - 1, NZ)}

    home = me // 4
    tile = lax.rem(me, 4)
    first_block = 3 * (tile // 2) + lax.rem(tile, 2)
    is_home = home == z

    my_chunk = lax.rem(me, 4)
    my_tile = me // 4
    home_x = 2 * lax.rem(z, 2) + 1
    home_y = z // 2
    last_tile = 2 * lax.rem(x + NX - home_x, NX) + core

    barrier = pltpu.get_barrier_semaphore()
    neighbours = [at(1, 0), at(-1, 0), at(0, 1), at(0, -1), sibling, above, below]
    for device in neighbours:
        pl.semaphore_signal(barrier, inc=1, device_id=device, device_id_type=MESH)

    b_copy = pltpu.make_async_copy(b_hbm, b_ref, local_sem.at[0])
    occ_copy = pltpu.make_async_copy(occ_hbm, occ_ref, local_sem.at[1])
    own_copies = [
        pltpu.make_async_copy(
            v_hbm.at[:, pl.ds(k * CHUNK, CHUNK)], panel.at[k, pl.ds(me * nrows, nrows)], local_sem.at[2 + k]
        )
        for k in range(nchunks)
    ]
    for copy in own_copies:
        copy.start()
    b_copy.start()
    occ_copy.start()

    pl.semaphore_wait(barrier, len(neighbours))

    def z_signal(r):
        for device in (above, below):
            pl.semaphore_signal(z_token.at[r], inc=1, device_id=device, device_id_type=MESH)

    def z_wait(r):
        pl.semaphore_wait(z_token.at[r], 2)

    half = nrows // 32 * 16 + 16 if nrows % 32 else nrows // 2

    def push(k, row, count, device, slot, src=None):
        block = panel.at[k, pl.ds(row, count)]
        pltpu.make_async_remote_copy(
            src_ref=block if src is None else src,
            dst_ref=block,
            send_sem=send_sem.at[k],
            recv_sem=recv_sem.at[k, slot],
            device_id=device,
            device_id_type=MESH,
        ).start()

    def row_of(f, s):
        return pl.multiple_of(occ_of(f, s) * nrows, 16)

    def shard(k, f, s, device, slot):
        push(k, row_of(f, s), nrows, device, slot)

    def arrived(k, slot, count):
        block = panel.at[k, pl.ds(0, count)]
        pltpu.make_async_copy(block, block, recv_sem.at[k, slot]).wait()

    def phase0(k):
        src = v_hbm.at[:, pl.ds(k * CHUNK, CHUNK)]
        row = row_of(0, 0)
        push(k, row, nrows, at(1, 0), 0, src)
        push(k, row, nrows, at(-1, 0), 1, src)
        push(k, row, nrows, sibling, 10, src)

    def halves(k):
        arrived(k, 0, nrows)
        push(k, row_of(-1, 0), half, at(1, 0), 2)
        arrived(k, 1, nrows)
        push(k, pl.multiple_of(row_of(1, 0) + half, 16), nrows - half, at(-1, 0), 3)

    def bulk(k):
        own_copies[k].wait()
        shard(k, 1, 0, at(0, -1), 6)
        for f in (0, -1):
            shard(k, f, 0, at(0, 1), 4)
        for f in (0, -1):
            shard(k, f, 0, at(0, -1), 7)
        shard(k, 1, 0, at(0, 1), 5)
        shard(k, 1, 0, sibling, 10)
        shard(k, -1, 0, sibling, 10)

    def opposite(k):
        arrived(k, 2, half)
        arrived(k, 3, nrows - half)
        shard(k, 2, 0, at(0, -1), 11)
        shard(k, 2, 0, at(0, 1), 5)
        shard(k, 2, 0, sibling, 10)

    def phase3(k):
        arrived(k, 4, 2 * nrows)
        for f in (0, -1):
            shard(k, f, -1, at(0, 1), 8)
        arrived(k, 6, nrows)
        shard(k, 1, 1, at(0, -1), 9)
        for f in (0, -1):
            shard(k, f, -1, sibling, 10)
        shard(k, 1, 1, sibling, 10)
        arrived(k, 11, nrows)
        shard(k, 2, 1, at(0, -1), 9)
        shard(k, 2, 1, sibling, 10)
        arrived(k, 5, 2 * nrows)
        for f in (1, 2):
            shard(k, f, -1, sibling, 10)
        arrived(k, 7, 2 * nrows)
        for f in (0, -1):
            shard(k, f, 1, sibling, 10)

    def phase4(k):
        arrived(k, 8, 2 * nrows)
        for f in (0, -1):
            shard(k, f, 2, sibling, 10)
        arrived(k, 9, 2 * nrows)
        for f in (1, 2):
            shard(k, f, 2, sibling, 10)

    def phase5(k):
        arrived(k, 10, PLANE // 2 * nrows)

    def compute(k, g):
        depth = TILE_P * occ_local
        t = jnp.dot(b_ref[pl.ds(g * depth, depth), :], panel[k], preferred_element_type=jnp.float32)
        o = occ_ref[:, pl.ds(k * CHUNK, CHUNK)].astype(jnp.float32)
        sums = jnp.sum(t.reshape(TILE_P, occ_local, CHUNK) * o[None], axis=1)
        for h in range(blocks):
            part[k * blocks + h, pl.ds(g * TILE_P, TILE_P)] = sums[:, h * LANES:(h + 1) * LANES]

    def multiply(k):
        for g in range(groups):
            compute(k, g)

    def tile_of(ref, k, t):
        return ref.at[k * blocks + t // groups, pl.ds(pl.multiple_of(lax.rem(t, groups) * TILE_P, TILE_P), TILE_P)]

    def send(src, dst, ssem, rsem, occ, pts):
        pltpu.make_async_remote_copy(
            src_ref=src, dst_ref=dst, send_sem=ssem, recv_sem=rsem,
            device_id={"occ": occ, "pts": pts}, device_id_type=MESH,
        ).start()

    def send_part(k, t, owner):
        send(tile_of(part, k, t), gathered.at[k, lax.rem(me - owner + PLANE, PLANE) - 1],
             rs_send, rs_recv.at[k], owner, z)

    def scatter(k):
        def step(n, _):
            t = lax.rem(my_tile + n, tiles)
            send_part(k, t, t * 4 + k)
            return 0

        lax.fori_loop(jnp.where(my_chunk == k, 1, 0), tiles, step, 0)

    def scatter_last():
        def step(n, _):
            t = n // NY
            row = lax.rem(y + lax.rem(n, NY), NY)
            owner = (row * NX + lax.rem(home_x + t // 2, NX)) * 2 + lax.rem(t, 2)

            @pl.when(owner != me)
            def _():
                send_part(last, t, owner)

            return 0

        lax.fori_loop(0, tiles * NY, step, 0)

    def wait_tiles(sem, count):
        block = gathered.at[0, pl.ds(0, count)]
        pltpu.make_async_copy(block, block, sem).wait()

    def add_up(k, t):
        wait_tiles(rs_recv.at[k], PLANE - 1)
        acc = tile_of(part, k, t)[...]
        for n in range(PLANE - 1):
            acc = acc + gathered[k, n]
        total[k] = acc
        tile_of(rows_y, k, t)[...] = acc

    def to_columns(k, t):
        block = k * blocks + t // groups
        low = 2 * (block // 3) + lax.rem(block, 3) // 2
        count = jnp.where(lax.rem(block, 3) == 1, 2, 1)

        def step(n, _):
            user = low + n // (NZ - 1)
            slot = block - (3 * (user // 2) + lax.rem(user, 2))
            send(total.at[k],
                 cols_y.at[slot, pl.ds(pl.multiple_of(lax.rem(t, groups) * TILE_P, TILE_P), TILE_P)],
                 ag_send, col_recv, z * 4 + user, lax.rem(z + 1 + lax.rem(n, NZ - 1), NZ))
            return 0

        lax.fori_loop(0, count * (NZ - 1), step, 0)

    def spread(k):
        add_up(k, my_tile)
        to_columns(k, my_tile)

        def step(n, _):
            send(total.at[k], tile_of(rows_y, k, my_tile), ag_send, ag_recv.at[k], lax.rem(me + n, PLANE), z)
            return 0

        lax.fori_loop(1, PLANE, step, 0)

    def spread_last():
        add_up(last, last_tile)

        @pl.when(y == home_y)
        def _():
            to_columns(last, last_tile)

        def step(n, _):
            send(total.at[last], tile_of(rows_y, last, last_tile), ag_send, ag_recv.at[last],
                 y * 2 * NX + lax.rem(x * 2 + core + n, 2 * NX), z)
            return 0

        lax.fori_loop(1, 2 * NX, step, 0)

    def columns_sent(k, t):
        wait_tiles(ag_send, NZ - 1)

        @pl.when(lax.rem(k * blocks + t // groups, 3) == 1)
        def _():
            wait_tiles(ag_send, NZ - 1)

    z_signal(0)
    for k in range(nchunks):
        phase0(k)
    halves(0)
    bulk(0)
    halves(1)
    halves(2)
    z_wait(0)
    z_signal(1)
    opposite(0)
    bulk(1)
    opposite(1)
    opposite(2)
    phase3(0)
    z_wait(1)
    z_signal(2)
    bulk(2)
    phase3(1)
    b_copy.wait()
    occ_copy.wait()
    phase4(0)
    phase5(0)
    multiply(0)
    z_wait(2)
    scatter(0)
    phase3(2)
    phase4(1)
    phase5(1)
    multiply(1)
    scatter(1)
    phase4(2)
    phase5(2)
    multiply(2)
    scatter_last()

    for k in range(last):
        @pl.when(my_chunk == k)
        def _():
            spread(k)

    spread_last()

    for k in range(last):
        @pl.when(my_chunk == k)
        def _():
            wait_tiles(ag_recv.at[k], tiles - 1)

        @pl.when(my_chunk != k)
        def _():
            wait_tiles(ag_recv.at[k], tiles)

    wait_tiles(ag_recv.at[last], tiles - 1)

    @pl.when(is_home)
    def _():
        cols_y[...] = rows_y[pl.ds(first_block, 2)]

    @pl.when(jnp.logical_not(is_home))
    def _():
        wait_tiles(col_recv, 2 * groups)

    for k in range(nchunks):
        sent = panel.at[k, pl.ds(0, (PLANE - 1) * nrows)]
        pltpu.make_async_copy(sent, sent, send_sem.at[k]).wait()

    wait_tiles(rs_send, PLANE - 1)
    for k in range(last):
        @pl.when(my_chunk == k)
        def _():
            wait_tiles(rs_send, tiles - 1)
            wait_tiles(ag_send, PLANE - 1)
            columns_sent(k, my_tile)

        @pl.when(my_chunk != k)
        def _():
            wait_tiles(rs_send, tiles)

    wait_tiles(ag_send, tiles - 1)

    @pl.when(y == home_y)
    def _():
        columns_sent(last, last_tile)


def gram_kernel(rows_ref, cols_ref, out_ref):
    odd = lax.rem(lax.axis_index("occ"), 2) == 1
    cols = jnp.concatenate([cols_ref[0], cols_ref[1]], axis=1)
    cols = jnp.where(odd, pltpu.roll(cols, cols.shape[1] - LANES // 2, 1), cols)
    c1, c2, c3 = split3(cols)
    right = jnp.concatenate([c1, c2, c1, c2, c3, c1], axis=0)
    for qb in range(rows_ref.shape[0]):
        r1, r2, r3 = split3(rows_ref[qb])
        left = jnp.concatenate([r1, r1, r2, r2, r1, r3], axis=0)
        g = lax.dot_general(left, right, (((0,), (0,)), ((), ())), preferred_element_type=jnp.float32)
        out_ref[pl.ds(qb * LANES, LANES), :] = g[:, :out_ref.shape[1]]


def body(integrals, occupied_points, virtual_points):
    naux, occ_local, nvirt = integrals.shape
    nrows, width = virtual_points.shape
    nchunks = width // CHUNK
    tiles_q = width // LANES
    tile_width = width * NZ // PLANE
    flat = integrals.reshape(naux * occ_local, nvirt)
    anywhere = pl.BlockSpec(memory_space=pl.ANY)
    vmem = pl.BlockSpec(memory_space=pltpu.VMEM)
    rows, cols = pl.pallas_call(
        kernel,
        out_shape=[
            jax.ShapeDtypeStruct((tiles_q, naux, LANES), jnp.float32),
            jax.ShapeDtypeStruct((2, naux, LANES), jnp.float32),
        ],
        in_specs=[anywhere] * 3,
        out_specs=[vmem] * 2,
        scratch_shapes=[
            pltpu.VMEM((naux * occ_local, nvirt), jnp.bfloat16),
            pltpu.VMEM((occ_local, width), jnp.bfloat16),
            pltpu.VMEM((nchunks, nvirt, CHUNK), jnp.bfloat16),
            pltpu.VMEM((tiles_q, naux, LANES), jnp.float32),
            pltpu.VMEM((nchunks, PLANE, TILE_P, LANES), jnp.float32),
            pltpu.VMEM((nchunks, TILE_P, LANES), jnp.float32),
            pltpu.SemaphoreType.DMA((2 + nchunks,)),
            pltpu.SemaphoreType.DMA((nchunks, 12)),
            pltpu.SemaphoreType.DMA((nchunks,)),
            pltpu.SemaphoreType.DMA,
            pltpu.SemaphoreType.DMA((nchunks,)),
            pltpu.SemaphoreType.DMA,
            pltpu.SemaphoreType.DMA((nchunks,)),
            pltpu.SemaphoreType.DMA,
            pltpu.SemaphoreType.REGULAR((3,)),
        ],
        compiler_params=pltpu.CompilerParams(
            collective_id=0, has_side_effects=True, vmem_limit_bytes=56 * 2**20
        ),
        cost_estimate=pl.CostEstimate(
            flops=2 * naux * occ_local * nvirt * width, bytes_accessed=12 * 2**20, transcendentals=0
        ),
        name="project",
    )(flat, occupied_points, virtual_points)
    return pl.pallas_call(
        gram_kernel,
        out_shape=jax.ShapeDtypeStruct((width, tile_width), jnp.float32),
        in_specs=[vmem] * 2,
        out_specs=vmem,
        cost_estimate=pl.CostEstimate(
            flops=12 * naux * width * tile_width, bytes_accessed=2**20, transcendentals=0
        ),
        name="gram",
    )(rows, cols)


def solution(mesh):
    return jax.shard_map(
        body,
        mesh=mesh,
        in_specs=(P(None, "occ", None), P("occ", "pts"), P("occ", "pts")),
        out_specs=P("pts", "occ"),
        check_vma=False,
    )
```

time: 61.8 us -> 54 us (0.87)
  Pallas kernels: 59.4 us -> 51.6 us
    pallas_call x1 -> x2, Pallas kernels: 59.4 us -> 51.6 us  [the longest x1 49.5 us: body(): pl.pallas_call(kernel, out_shape=[jax.ShapeDtypeStruct((tiles_q, naux, LA...]
where the time goes in v2:
time: 54 us; the launch traced here: 53.9 us
  Pallas kernels  51.6 us (96%)
  local copies, waits for them, and re-layouts  2.2 us (4%)
    pallas_call x1, Pallas kernels, body(): pl.pallas_call(kernel, out_shape=[jax.ShapeDtypeStruct((tiles_q, naux, LA...  49.5 us
    pallas_call x1, local copies, waits for them, and re-layouts, body(): pl.pallas_call(gram_kernel, out_shape=jax.ShapeDtypeStruct((width, tile_w...  2.2 us
    pallas_call x1, Pallas kernels, body(): pl.pallas_call(gram_kernel, out_shape=jax.ShapeDtypeStruct((width, tile_w...  2.12 us

profile of v2, /device:TPU:1, one launch (start us, length us, event | category | flops | bytes accessed | tf_op | source)
XLA Modules:
  0.0 53.9 jit_solution(2597777532840024867)
XLA Ops:
  0.0 49.5 %project.1 = (f32[6,32,128]{2,1,0:T(8,128)}, f32[2,32,128]{2,1,0:T(8,128)}) custom-call(bf16[1024,4608]{1,0:T(8,128)(2,1)} %bitcast.1, bf16[32,768]{1,0:T(8,128)(2,1)} %occ_hbm.1, bf16[144,768]{1,0:T(8,128)(2,1)} %v_hbm.1), custom_call_target="tpu_custom_call" | custom-call | flops 7247757312 | bytes 12582912 | tf_op jit(solution)/shard_map/project/pallas_call | solution.py:390
  49.5 2.1 %gram.1 = f32[768,192]{1,0:T(8,128)} custom-call(f32[6,32,128]{2,1,0:T(8,128)} %get-tuple-element.7.rows_ref, f32[2,32,128]{2,1,0:T(8,128)} %get-tuple-element.8.cols_ref), custom_call_target="tpu_custom_call" | custom-call | flops 56623104 | bytes 1048576 | tf_op jit(solution)/shard_map/gram/pallas_call | solution.py:423
  51.7 2.2 %copy.4 = f32[768,192]{0,1:T(8,128)} copy(f32[768,192]{1,0:T(8,128)} %gram.1) | data formatting | bytes 1179648 | tf_op jit(solution)/shard_map/gram/pallas_call | solution.py:423

commit v3 on v2

--- a/solution.py
+++ b/solution.py
@@ -63,7 +63,11 @@
     my_tile = me // 4
     home_x = 2 * lax.rem(z, 2) + 1
     home_y = z // 2
-    last_tile = 2 * lax.rem(x + NX - home_x, NX) + core
+    home_dy = lax.rem(y + NY - home_y, NY)
+    last_tile = 2 * lax.rem(x + NX - home_x + 2 * home_dy, NX) + core
+    sends_columns = jnp.logical_or(
+        jnp.logical_and(home_dy == 0, last_tile // 2 != 2), jnp.logical_and(home_dy == 1, last_tile // 2 == 2)
+    )
 
     barrier = pltpu.get_barrier_semaphore()
     neighbours = [at(1, 0), at(-1, 0), at(0, 1), at(0, -1), sibling, above, below]
@@ -146,7 +150,7 @@
         shard(k, 2, 0, at(0, 1), 5)
         shard(k, 2, 0, sibling, 10)
 
-    def phase3(k):
+    def phase3a(k):
         arrived(k, 4, 2 * nrows)
         for f in (0, -1):
             shard(k, f, -1, at(0, 1), 8)
@@ -155,9 +159,13 @@
         for f in (0, -1):
             shard(k, f, -1, sibling, 10)
         shard(k, 1, 1, sibling, 10)
+
+    def phase3b(k):
         arrived(k, 11, nrows)
         shard(k, 2, 1, at(0, -1), 9)
         shard(k, 2, 1, sibling, 10)
+
+    def phase3c(k):
         arrived(k, 5, 2 * nrows)
         for f in (1, 2):
             shard(k, f, -1, sibling, 10)
@@ -165,13 +173,24 @@
         for f in (0, -1):
             shard(k, f, 1, sibling, 10)
 
-    def phase4(k):
+    def phase3(k):
+        phase3a(k)
+        phase3b(k)
+        phase3c(k)
+
+    def phase4a(k):
         arrived(k, 8, 2 * nrows)
         for f in (0, -1):
             shard(k, f, 2, sibling, 10)
+
+    def phase4b(k):
         arrived(k, 9, 2 * nrows)
         for f in (1, 2):
             shard(k, f, 2, sibling, 10)
+
+    def phase4(k):
+        phase4a(k)
+        phase4b(k)
 
     def phase5(k):
         arrived(k, 10, PLANE // 2 * nrows)
@@ -189,6 +208,8 @@
             compute(k, g)
 
     def tile_of(ref, k, t):
+        if isinstance(t, int):
+            return ref.at[k * blocks + t // groups, pl.ds(t % groups * TILE_P, TILE_P)]
         return ref.at[k * blocks + t // groups, pl.ds(pl.multiple_of(lax.rem(t, groups) * TILE_P, TILE_P), TILE_P)]
 
     def send(src, dst, ssem, rsem, occ, pts):
@@ -209,19 +230,19 @@
 
         lax.fori_loop(jnp.where(my_chunk == k, 1, 0), tiles, step, 0)
 
-    def scatter_last():
-        def step(n, _):
-            t = n // NY
-            row = lax.rem(y + lax.rem(n, NY), NY)
-            owner = (row * NX + lax.rem(home_x + t // 2, NX)) * 2 + lax.rem(t, 2)
-
-            @pl.when(owner != me)
-            def _():
-                send_part(last, t, owner)
-
-            return 0
-
-        lax.fori_loop(0, tiles * NY, step, 0)
+    def scatter_last(first_group, last_group):
+        for t in range(tiles):
+            if not first_group <= t % groups < last_group:
+                continue
+            for r in range(NY):
+                column = lax.rem(home_x + t // 2 + 2 * (home_dy + r), NX)
+                owner = (lax.rem(y + r, NY) * NX + column) * 2 + t % 2
+                if r:
+                    send_part(last, t, owner)
+                else:
+                    @pl.when(last_tile != t)
+                    def _():
+                        send_part(last, t, owner)
 
     def wait_tiles(sem, count):
         block = gathered.at[0, pl.ds(0, count)]
@@ -263,7 +284,7 @@
     def spread_last():
         add_up(last, last_tile)
 
-        @pl.when(y == home_y)
+        @pl.when(sends_columns)
         def _():
             to_columns(last, last_tile)
 
@@ -282,39 +303,49 @@
             wait_tiles(ag_send, NZ - 1)
 
     z_signal(0)
-    for k in range(nchunks):
-        phase0(k)
+    phase0(0)
+    phase0(1)
+    phase0(2)
     halves(0)
     bulk(0)
     halves(1)
     halves(2)
+    bulk(1)
     z_wait(0)
     z_signal(1)
     opposite(0)
-    bulk(1)
     opposite(1)
     opposite(2)
     phase3(0)
     z_wait(1)
     z_signal(2)
+    phase3(1)
     bulk(2)
-    phase3(1)
     b_copy.wait()
     occ_copy.wait()
     phase4(0)
     phase5(0)
-    multiply(0)
+    compute(0, 0)
+    compute(0, 1)
+    compute(0, 2)
+    compute(0, 3)
+    phase3a(2)
+    phase3b(2)
+    phase3c(2)
+    phase4(1)
     z_wait(2)
     scatter(0)
-    phase3(2)
-    phase4(1)
     phase5(1)
-    multiply(1)
+    compute(1, 0)
+    compute(1, 1)
+    phase4a(2)
+    phase4b(2)
+    compute(1, 2)
+    compute(1, 3)
+    phase5(2)
     scatter(1)
-    phase4(2)
-    phase5(2)
     multiply(2)
-    scatter_last()
+    scatter_last(0, groups)
 
     for k in range(last):
         @pl.when(my_chunk == k)
@@ -360,7 +391,7 @@
 
     wait_tiles(ag_send, tiles - 1)
 
-    @pl.when(y == home_y)
+    @pl.when(sends_columns)
     def _():
         columns_sent(last, last_tile)
 
@@ -374,8 +405,8 @@
     for qb in range(rows_ref.shape[0]):
         r1, r2, r3 = split3(rows_ref[qb])
         left = jnp.concatenate([r1, r1, r2, r2, r1, r3], axis=0)
-        g = lax.dot_general(left, right, (((0,), (0,)), ((), ())), preferred_element_type=jnp.float32)
-        out_ref[pl.ds(qb * LANES, LANES), :] = g[:, :out_ref.shape[1]]
+        g = lax.dot_general(right, left, (((0,), (0,)), ((), ())), preferred_element_type=jnp.float32)
+        out_ref[:, pl.ds(qb * LANES, LANES)] = g[:out_ref.shape[0]]
 
 
 def body(integrals, occupied_points, virtual_points):
@@ -420,9 +451,9 @@
         ),
         name="project",
     )(flat, occupied_points, virtual_points)
-    return pl.pallas_call(
+    transposed = pl.pallas_call(
         gram_kernel,
-        out_shape=jax.ShapeDtypeStruct((width, tile_width), jnp.float32),
+        out_shape=jax.ShapeDtypeStruct((tile_width, width), jnp.float32),
         in_specs=[vmem] * 2,
         out_specs=vmem,
         cost_estimate=pl.CostEstimate(
@@ -430,6 +461,7 @@
         ),
         name="gram",
     )(rows, cols)
+    return transposed.T
 
 
 def solution(mesh):

time: 54 us -> 50.4 us (0.933)
  local copies, waits for them, and re-layouts: 2.2 us -> 0 us
  Pallas kernels: 51.6 us -> 50.3 us
    pallas_call x1 -> x0, local copies, waits for them, and re-layouts: 2.2 us -> none  [body(): pl.pallas_call(gram_kernel, out_shape=jax.ShapeDtypeStruct((width, tile_w...]
    pallas_call x1, Pallas kernels: 49.5 us -> 48.1 us  [body(): pl.pallas_call(kernel, out_shape=[jax.ShapeDtypeStruct((tiles_q, naux, LA...]
where the time goes in v3:
time: 50.4 us; the launch traced here: 50.3 us
  Pallas kernels  50.3 us (100%)
    pallas_call x1, Pallas kernels, body(): pl.pallas_call(kernel, out_shape=[jax.ShapeDtypeStruct((tiles_q, naux, LA...  48.1 us
    pallas_call x1, Pallas kernels, body(): pl.pallas_call(gram_kernel, out_shape=jax.ShapeDtypeStruct((tile_width, w...  2.16 us

profile of v3, /device:TPU:1, one launch (start us, length us, event | category | flops | bytes accessed | tf_op | source)
XLA Modules:
  0.0 50.3 jit_solution(14400880027507036468)
XLA Ops:
  0.0 48.1 %project.1 = (f32[6,32,128]{2,1,0:T(8,128)}, f32[2,32,128]{2,1,0:T(8,128)}) custom-call(bf16[1024,4608]{1,0:T(8,128)(2,1)} %bitcast.2, bf16[32,768]{1,0:T(8,128)(2,1)} %occ_hbm.1, bf16[144,768]{1,0:T(8,128)(2,1)} %v_hbm.1), custom_call_target="tpu_custom_call" | custom-call | flops 7247757312 | bytes 12582912 | tf_op jit(solution)/shard_map/project/pallas_call | solution.py:421
  48.1 2.2 %gram.1 = f32[192,768]{1,0:T(8,128)} custom-call(f32[6,32,128]{2,1,0:T(8,128)} %get-tuple-element.7.rows_ref, f32[2,32,128]{2,1,0:T(8,128)} %get-tuple-element.8.cols_ref), custom_call_target="tpu_custom_call" | custom-call | flops 56623104 | bytes 1048576 | tf_op jit(solution)/shard_map/gram/pallas_call | solution.py:454

commit v4 on v3

--- a/solution.py
+++ b/solution.py
@@ -84,8 +84,6 @@
     ]
     for copy in own_copies:
         copy.start()
-    b_copy.start()
-    occ_copy.start()
 
     pl.semaphore_wait(barrier, len(neighbours))
 
@@ -98,10 +96,10 @@
 
     half = nrows // 32 * 16 + 16 if nrows % 32 else nrows // 2
 
-    def push(k, row, count, device, slot, src=None):
+    def push(k, row, count, device, slot):
         block = panel.at[k, pl.ds(row, count)]
         pltpu.make_async_remote_copy(
-            src_ref=block if src is None else src,
+            src_ref=block,
             dst_ref=block,
             send_sem=send_sem.at[k],
             recv_sem=recv_sem.at[k, slot],
@@ -120,11 +118,10 @@
         pltpu.make_async_copy(block, block, recv_sem.at[k, slot]).wait()
 
     def phase0(k):
-        src = v_hbm.at[:, pl.ds(k * CHUNK, CHUNK)]
-        row = row_of(0, 0)
-        push(k, row, nrows, at(1, 0), 0, src)
-        push(k, row, nrows, at(-1, 0), 1, src)
-        push(k, row, nrows, sibling, 10, src)
+        own_copies[k].wait()
+        shard(k, 0, 0, at(1, 0), 0)
+        shard(k, 0, 0, at(-1, 0), 1)
+        shard(k, 0, 0, sibling, 10)
 
     def halves(k):
         arrived(k, 0, nrows)
@@ -133,7 +130,6 @@
         push(k, pl.multiple_of(row_of(1, 0) + half, 16), nrows - half, at(-1, 0), 3)
 
     def bulk(k):
-        own_copies[k].wait()
         shard(k, 1, 0, at(0, -1), 6)
         for f in (0, -1):
             shard(k, f, 0, at(0, 1), 4)
@@ -234,7 +230,7 @@
         for t in range(tiles):
             if not first_group <= t % groups < last_group:
                 continue
-            for r in range(NY):
+            for r in (2, 1, 3, 0):
                 column = lax.rem(home_x + t // 2 + 2 * (home_dy + r), NX)
                 owner = (lax.rem(y + r, NY) * NX + column) * 2 + t % 2
                 if r:
@@ -259,17 +255,19 @@
     def to_columns(k, t):
         block = k * blocks + t // groups
         low = 2 * (block // 3) + lax.rem(block, 3) // 2
-        count = jnp.where(lax.rem(block, 3) == 1, 2, 1)
-
-        def step(n, _):
-            user = low + n // (NZ - 1)
+
+        def to_user(user):
             slot = block - (3 * (user // 2) + lax.rem(user, 2))
-            send(total.at[k],
-                 cols_y.at[slot, pl.ds(pl.multiple_of(lax.rem(t, groups) * TILE_P, TILE_P), TILE_P)],
-                 ag_send, col_recv, z * 4 + user, lax.rem(z + 1 + lax.rem(n, NZ - 1), NZ))
-            return 0
-
-        lax.fori_loop(0, count * (NZ - 1), step, 0)
+            for n in (4, 3, 5, 2, 6, 1, 7):
+                send(total.at[k],
+                     cols_y.at[slot, pl.ds(pl.multiple_of(lax.rem(t, groups) * TILE_P, TILE_P), TILE_P)],
+                     ag_send, col_recv, z * 4 + user, lax.rem(z + n, NZ))
+
+        to_user(low)
+
+        @pl.when(lax.rem(block, 3) == 1)
+        def _():
+            to_user(low + 1)
 
     def spread(k):
         add_up(k, my_tile)
@@ -306,29 +304,28 @@
     phase0(0)
     phase0(1)
     phase0(2)
+    b_copy.start()
+    occ_copy.start()
     halves(0)
     bulk(0)
     halves(1)
+    bulk(1)
     halves(2)
-    bulk(1)
+    opposite(0)
+    opposite(1)
     z_wait(0)
     z_signal(1)
-    opposite(0)
-    opposite(1)
+    phase3(0)
     opposite(2)
-    phase3(0)
+    bulk(2)
+    phase3(1)
     z_wait(1)
     z_signal(2)
-    phase3(1)
-    bulk(2)
     b_copy.wait()
     occ_copy.wait()
     phase4(0)
     phase5(0)
-    compute(0, 0)
-    compute(0, 1)
-    compute(0, 2)
-    compute(0, 3)
+    multiply(0)
     phase3a(2)
     phase3b(2)
     phase3c(2)

time: 50.4 us -> 48.9 us (0.970)
  Pallas kernels: 50.3 us -> 48.8 us
    pallas_call x1, Pallas kernels: 48.1 us -> 46.6 us  [body(): pl.pallas_call(kernel, out_shape=[jax.ShapeDtypeStruct((tiles_q, naux, LA...]
where the time goes in v4:
time: 48.9 us; the launch traced here: 48.8 us
  Pallas kernels  48.8 us (100%)
    pallas_call x1, Pallas kernels, body(): pl.pallas_call(kernel, out_shape=[jax.ShapeDtypeStruct((tiles_q, naux, LA...  46.6 us
    pallas_call x1, Pallas kernels, body(): pl.pallas_call(gram_kernel, out_shape=jax.ShapeDtypeStruct((tile_width, w...  2.16 us

profile of v4, /device:TPU:1, one launch (start us, length us, event | category | flops | bytes accessed | tf_op | source)
XLA Modules:
  0.0 48.8 jit_solution(52363456568203371)
XLA Ops:
  0.0 46.6 %project.1 = (f32[6,32,128]{2,1,0:T(8,128)}, f32[2,32,128]{2,1,0:T(8,128)}) custom-call(bf16[1024,4608]{1,0:T(8,128)(2,1)} %bitcast.2, bf16[32,768]{1,0:T(8,128)(2,1)} %occ_hbm.1, bf16[144,768]{1,0:T(8,128)(2,1)} %v_hbm.1), custom_call_target="tpu_custom_call" | custom-call | flops 7247757312 | bytes 12582912 | tf_op jit(solution)/shard_map/project/pallas_call | solution.py:418
  46.6 2.2 %gram.1 = f32[192,768]{1,0:T(8,128)} custom-call(f32[6,32,128]{2,1,0:T(8,128)} %get-tuple-element.7.rows_ref, f32[2,32,128]{2,1,0:T(8,128)} %get-tuple-element.8.cols_ref), custom_call_target="tpu_custom_call" | custom-call | flops 56623104 | bytes 1048576 | tf_op jit(solution)/shard_map/gram/pallas_call | solution.py:451

commit v5 on v4

--- a/solution.py
+++ b/solution.py
@@ -13,6 +13,7 @@
 CHUNK = 256
 LANES = 128
 TILE_P = 8
+REPLICAS = 2
 
 
 def split3(x):
@@ -65,6 +66,7 @@
     home_y = z // 2
     home_dy = lax.rem(y + NY - home_y, NY)
     last_tile = 2 * lax.rem(x + NX - home_x + 2 * home_dy, NX) + core
+    owns_last = home_dy < REPLICAS
     sends_columns = jnp.logical_or(
         jnp.logical_and(home_dy == 0, last_tile // 2 != 2), jnp.logical_and(home_dy == 1, last_tile // 2 == 2)
     )
@@ -226,19 +228,15 @@
 
         lax.fori_loop(jnp.where(my_chunk == k, 1, 0), tiles, step, 0)
 
-    def scatter_last(first_group, last_group):
-        for t in range(tiles):
-            if not first_group <= t % groups < last_group:
-                continue
-            for r in (2, 1, 3, 0):
-                column = lax.rem(home_x + t // 2 + 2 * (home_dy + r), NX)
-                owner = (lax.rem(y + r, NY) * NX + column) * 2 + t % 2
-                if r:
+    def scatter_last():
+        for d in range(REPLICAS):
+            for t in range(tiles):
+                column = lax.rem(home_x + t // 2 + 2 * d, NX)
+                owner = (lax.rem(home_y + d, NY) * NX + column) * 2 + t % 2
+
+                @pl.when(owner != me)
+                def _():
                     send_part(last, t, owner)
-                else:
-                    @pl.when(last_tile != t)
-                    def _():
-                        send_part(last, t, owner)
 
     def wait_tiles(sem, count):
         block = gathered.at[0, pl.ds(0, count)]
@@ -286,12 +284,13 @@
         def _():
             to_columns(last, last_tile)
 
-        def step(n, _):
-            send(total.at[last], tile_of(rows_y, last, last_tile), ag_send, ag_recv.at[last],
-                 y * 2 * NX + lax.rem(x * 2 + core + n, 2 * NX), z)
-            return 0
-
-        lax.fori_loop(1, 2 * NX, step, 0)
+        for row in range(NY // REPLICAS - 1, -1, -1):
+            def step(n, _):
+                send(total.at[last], tile_of(rows_y, last, last_tile), ag_send, ag_recv.at[last],
+                     lax.rem(y + row * REPLICAS, NY) * 2 * NX + lax.rem(x * 2 + core + n, 2 * NX), z)
+                return 0
+
+            lax.fori_loop(0 if row else 1, 2 * NX, step, 0)
 
     def columns_sent(k, t):
         wait_tiles(ag_send, NZ - 1)
@@ -330,8 +329,6 @@
     phase3b(2)
     phase3c(2)
     phase4(1)
-    z_wait(2)
-    scatter(0)
     phase5(1)
     compute(1, 0)
     compute(1, 1)
@@ -339,17 +336,21 @@
     phase4b(2)
     compute(1, 2)
     compute(1, 3)
+    z_wait(2)
+    scatter(0)
+    scatter(1)
     phase5(2)
-    scatter(1)
     multiply(2)
-    scatter_last(0, groups)
+    scatter_last()
 
     for k in range(last):
         @pl.when(my_chunk == k)
         def _():
             spread(k)
 
-    spread_last()
+    @pl.when(owns_last)
+    def _():
+        spread_last()
 
     for k in range(last):
         @pl.when(my_chunk == k)
@@ -360,7 +361,13 @@
         def _():
             wait_tiles(ag_recv.at[k], tiles)
 
-    wait_tiles(ag_recv.at[last], tiles - 1)
+    @pl.when(owns_last)
+    def _():
+        wait_tiles(ag_recv.at[last], tiles - 1)
+
+    @pl.when(jnp.logical_not(owns_last))
+    def _():
+        wait_tiles(ag_recv.at[last], tiles)
 
     @pl.when(is_home)
     def _():
@@ -374,7 +381,15 @@
         sent = panel.at[k, pl.ds(0, (PLANE - 1) * nrows)]
         pltpu.make_async_copy(sent, sent, send_sem.at[k]).wait()
 
-    wait_tiles(rs_send, PLANE - 1)
+    @pl.when(owns_last)
+    def _():
+        wait_tiles(rs_send, REPLICAS * tiles - 1)
+        wait_tiles(ag_send, NY // REPLICAS * tiles - 1)
+
+    @pl.when(jnp.logical_not(owns_last))
+    def _():
+        wait_tiles(rs_send, REPLICAS * tiles)
+
     for k in range(last):
         @pl.when(my_chunk == k)
         def _():
@@ -385,8 +400,6 @@
         @pl.when(my_chunk != k)
         def _():
             wait_tiles(rs_send, tiles)
-
-    wait_tiles(ag_send, tiles - 1)
 
     @pl.when(sends_columns)
     def _():
@@ -398,12 +411,12 @@
     cols = jnp.concatenate([cols_ref[0], cols_ref[1]], axis=1)
     cols = jnp.where(odd, pltpu.roll(cols, cols.shape[1] - LANES // 2, 1), cols)
     c1, c2, c3 = split3(cols)
-    right = jnp.concatenate([c1, c2, c1, c2, c3, c1], axis=0)
-    for qb in range(rows_ref.shape[0]):
-        r1, r2, r3 = split3(rows_ref[qb])
+    right = jnp.concatenate([c1, c2, c1, c2, c3, c1], axis=0).T[:out_ref.shape[0]]
+    for qb in range(0, rows_ref.shape[0], 2):
+        r1, r2, r3 = split3(jnp.concatenate([rows_ref[qb], rows_ref[qb + 1]], axis=1))
         left = jnp.concatenate([r1, r1, r2, r2, r1, r3], axis=0)
-        g = lax.dot_general(right, left, (((0,), (0,)), ((), ())), preferred_element_type=jnp.float32)
-        out_ref[:, pl.ds(qb * LANES, LANES)] = g[:out_ref.shape[0]]
+        g = jnp.dot(right, left, preferred_element_type=jnp.float32)
+        out_ref[:, pl.ds(qb * LANES, 2 * LANES)] = g
 
 
 def body(integrals, occupied_points, virtual_points):

time: 48.9 us -> 48.7 us (level)
  no operation moved by 1% of the time
where the time goes in v5:
time: 48.7 us; the launch traced here: 48.6 us
  Pallas kernels  48.6 us (100%)
    pallas_call x1, Pallas kernels, body(): pl.pallas_call(kernel, out_shape=[jax.ShapeDtypeStruct((tiles_q, naux, LA...  46.5 us
    pallas_call x1, Pallas kernels, body(): pl.pallas_call(gram_kernel, out_shape=jax.ShapeDtypeStruct((tile_width, w...  2.06 us

profile of v5, /device:TPU:1, one launch (start us, length us, event | category | flops | bytes accessed | tf_op | source)
XLA Modules:
  0.0 48.6 jit_solution(751290598594908782)
XLA Ops:
  0.0 46.5 %project.1 = (f32[6,32,128]{2,1,0:T(8,128)}, f32[2,32,128]{2,1,0:T(8,128)}) custom-call(bf16[1024,4608]{1,0:T(8,128)(2,1)} %bitcast.2, bf16[32,768]{1,0:T(8,128)(2,1)} %occ_hbm.1, bf16[144,768]{1,0:T(8,128)(2,1)} %v_hbm.1), custom_call_target="tpu_custom_call" | custom-call | flops 7247757312 | bytes 12582912 | tf_op jit(solution)/shard_map/project/pallas_call | solution.py:431
  46.5 2.1 %gram.1 = f32[192,768]{1,0:T(8,128)} custom-call(f32[6,32,128]{2,1,0:T(8,128)} %get-tuple-element.7.rows_ref, f32[2,32,128]{2,1,0:T(8,128)} %get-tuple-element.8.cols_ref), custom_call_target="tpu_custom_call" | custom-call | flops 56623104 | bytes 1048576 | tf_op jit(solution)/shard_map/gram/pallas_call | solution.py:464
